TPU v7x, 1024 devices: a whole 4x4x32 slice. The times are simulated.
1024 devices in a mesh: seq: 128 (over y, z), inner: 8 (over x, core).
Axes of the slice: x: 4, y: 4, z: 32, core: 2. Of those that a mesh axis runs over, the one named last changes fastest.
Arguments:
- queries: bfloat16 [8, 16, 262144], P('inner', None, 'seq'), may hold values from -24 to 24
- key_states: bfloat16 [8, 16, 262144], P('inner', None, 'seq'), may hold values from -24 to 24
- value_states: bfloat16 [128, 25, 262144], P('inner', None, 'seq'), may hold values from -48 to 48
- fractional: float32 [3, 262144], P(None, 'seq'), may hold values from 0 to 1
- block_counts: int32 [1024], replicated, may hold values from 64 to 256
- neighbors: int32 [1024, 3], P('seq'), may hold values from 0 to 1023, as said below
- integer_wave_vectors: int32 [3, 2048], replicated, may hold values from -7 to 7, as said below
- charge_weight: bfloat16 [128, 16], P('inner'), may hold values from -0.5 to 0.5
Outputs:
- attention: bfloat16 [128, 25, 262144], P('inner', None, 'seq')
- potential: float32 [16, 262144], P(None, 'seq')
- forces: float32 [3, 262144], P(None, 'seq')
Inputs may be any that keep to these rules, and one draw needn't show every extreme that they name: `neighbors`: row g lists 3 different blocks from g - 2 to g + 2 that lie in the grid, g itself among them. `integer_wave_vectors`: no column is all zeros.
All inputs are finite; a program needn't handle non-finite values.
Results may differ from a plain program's by a relative error of at most 0.006.
Values may be sent and summed in bfloat16 or wider, within the bound.
A program may use at most 32 MiB of HBM per device.

v0:
```python
import math

import jax
import jax.numpy as jnp
from jax import lax
from jax.sharding import Mesh
from jax.sharding import PartitionSpec as P

BS = 256
NNB = 3
SEQ = ("seq_0", "seq_1")


ewald_scale = 40.0
ewald_damp = 0.02


def padded(cells, sides, width):
    for axis, dim in sides:
        count = lax.axis_size(axis)
        ends = count - 1
        head = lax.slice_in_dim(cells, 0, width, axis=dim)
        tail = lax.slice_in_dim(cells, cells.shape[dim] - width, cells.shape[dim], axis=dim)
        cells = jnp.concatenate(
            [
                lax.ppermute(tail, axis, [(i, (i + 1) % count) for i in range(ends)]),
                cells,
                lax.ppermute(head, axis, [((i + 1) % count, i) for i in range(ends)]),
            ],
            axis=dim,
        )
    return cells


def sent_to_all(value, axis):
    length = lax.axis_size(axis)
    return lax.all_to_all(
        jnp.broadcast_to(value[None], (length, *value.shape)), axis, 0, 0, tiled=True
    )


def of_everyone(value, axis):
    return sent_to_all(value, axis).sum(axis=0)


def over_axes(value, axes):
    for axis in axes:
        value = lax.psum(value, axis)
    return value


def packed_total(arrays, axis):
    ends = [0]
    for a in arrays:
        ends.append(ends[-1] + a.size)
    subtotal = of_everyone(jnp.concatenate([a.ravel() for a in arrays]), axis)
    return tuple((subtotal[b:e].reshape(a.shape) for a, b, e in zip(arrays, ends, ends[1:])))


def attend_block(query_block, gathered, valid_keys, own_count, head_dim):
    key_part = gathered[:, :head_dim]
    value_part = gathered[:, head_dim:]
    scores = jnp.einsum(
        "hdq,hdk->hqk", query_block, key_part, preferred_element_type=jnp.float32
    ) * head_dim ** (-0.5)
    scores = jnp.where(valid_keys[None, None, :], scores, -jnp.inf)
    row_max = jnp.max(scores, axis=2, keepdims=True)
    weights = jnp.exp(scores - row_max)
    denominator = jnp.sum(weights, axis=2)
    mixture = (
        jnp.einsum(
            "hck,hqk->hcq",
            value_part,
            weights.astype(jnp.bfloat16),
            preferred_element_type=jnp.float32,
        )
        / denominator[:, None, :]
    )
    live_rows = jnp.arange(query_block.shape[2]) < own_count
    return jnp.where(live_rows[None, None, :], mixture, 0.0).astype(jnp.bfloat16)


def plane_wave_terms(reciprocal_vectors, atom_positions):
    phase_angles = (
        2.0
        * math.pi
        * (
            reciprocal_vectors[0][:, None] * atom_positions[0][None, :]
            + reciprocal_vectors[1][:, None] * atom_positions[1][None, :]
            + reciprocal_vectors[2][:, None] * atom_positions[2][None, :]
        )
    )
    return (jnp.cos(phase_angles), jnp.sin(phase_angles))


def contract(atom_charges, wave_table):
    return lax.dot_general(
        atom_charges,
        wave_table,
        (((1,), (1,)), ((), ())),
        precision=lax.Precision.HIGHEST,
        preferred_element_type=jnp.float32,
    )


def potential_field_values(
    atom_charges,
    cosine_phase_values,
    sine_phase_values,
    reciprocal_vectors,
    reciprocal_weight,
    structure_real,
    structure_imaginary,
):
    query_block_count = structure_real.shape[0]
    wave_vector_count = structure_real.shape[1]
    weighted_real_part = structure_real * reciprocal_weight[None, :]
    weighted_imaginary = structure_imaginary * reciprocal_weight[None, :]
    cosine_product = jnp.concatenate(
        [
            weighted_real_part,
            -(weighted_imaginary[None] * reciprocal_vectors[:, None, :]).reshape(
                3 * query_block_count, wave_vector_count
            ),
        ],
        axis=0,
    )
    sine_product = jnp.concatenate(
        [
            weighted_imaginary,
            (weighted_real_part[None] * reciprocal_vectors[:, None, :]).reshape(
                3 * query_block_count, wave_vector_count
            ),
        ],
        axis=0,
    )
    combined = jnp.dot(
        cosine_product,
        cosine_phase_values,
        precision=lax.Precision.HIGHEST,
        preferred_element_type=jnp.float32,
    ) + jnp.dot(
        sine_product,
        sine_phase_values,
        precision=lax.Precision.HIGHEST,
        preferred_element_type=jnp.float32,
    )
    potential = combined[:query_block_count]
    gradient = combined[query_block_count:].reshape(3, query_block_count, -1)
    forces = jnp.sum(atom_charges[None] * gradient, axis=1)
    return (potential, forces)


def local(
    queries,
    key_states,
    value_states,
    fractional,
    block_counts,
    neighbors,
    integer_wave_vectors,
    charge_weight,
):
    heads_here = queries.shape[0]
    head_dim = queries.shape[1]
    atoms_here = queries.shape[2]
    chans_here = value_states.shape[0]
    components = value_states.shape[1]
    head_chan = chans_here // heads_here
    row_width = head_dim + head_chan * components
    blocks_here = atoms_here // BS
    stacked = jnp.concatenate(
        [key_states, value_states.reshape(heads_here, head_chan * components, atoms_here)], axis=1
    )
    banded = padded(stacked, ((SEQ, 2),), 2 * BS)
    banded = banded.reshape(heads_here, row_width, blocks_here + 4, BS)
    device = lax.axis_index(SEQ)
    first_global = device * blocks_here
    padded_counts = jnp.pad(block_counts, (2, 2))
    band_counts = lax.dynamic_slice_in_dim(padded_counts, first_global, blocks_here + 4, 0)
    own_counts = lax.dynamic_slice_in_dim(block_counts, first_global, blocks_here, 0)
    slot_ids = jnp.arange(BS)
    band_valid = slot_ids[None, :] < band_counts[:, None]
    local_lists = neighbors - (first_global - 2)
    query_blocks = queries.reshape(heads_here, head_dim, blocks_here, BS).transpose(2, 0, 1, 3)

    def one_block(inputs):
        query_block, listed, own_count = inputs
        gathered = jnp.take(banded, listed, axis=2).reshape(heads_here, row_width, NNB * BS)
        valid_keys = jnp.take(band_valid, listed, axis=0).reshape(NNB * BS)
        return attend_block(query_block, gathered, valid_keys, own_count, head_dim)

    blocks_out = lax.map(one_block, (query_blocks, local_lists, own_counts))
    attention = blocks_out.transpose(1, 2, 0, 3).reshape(chans_here, components, atoms_here)
    partial_charges = lax.dot_general(
        charge_weight,
        attention[:, 0, :],
        (((0,), (0,)), ((), ())),
        preferred_element_type=jnp.float32,
    )
    reciprocal_vectors = integer_wave_vectors.astype(jnp.float32)
    squared_norm = jnp.sum(reciprocal_vectors * reciprocal_vectors, axis=0)
    reciprocal_weight = ewald_scale * jnp.exp(-ewald_damp * squared_norm) / squared_norm
    inner_block_count = lax.axis_size("inner")
    inner_block_index = lax.axis_index("inner")
    inv_root = 1.0 / math.sqrt(atoms_here * lax.axis_size(SEQ))
    atom_charges = of_everyone(partial_charges, "inner")
    local_atom_count = reciprocal_vectors.shape[1] // inner_block_count
    local_wave_vectors = lax.dynamic_slice_in_dim(
        reciprocal_vectors, inner_block_index * local_atom_count, local_atom_count, 1
    )
    own_weight = lax.dynamic_slice_in_dim(
        reciprocal_weight, inner_block_index * local_atom_count, local_atom_count, 0
    )
    cosine_phase_values, sine_phase_values = plane_wave_terms(local_wave_vectors, fractional)
    part_real = contract(atom_charges, cosine_phase_values) * inv_root
    part_imag = contract(atom_charges, sine_phase_values) * inv_root
    structure_real, structure_imaginary = (over_axes(part_real, SEQ), over_axes(part_imag, SEQ))
    potential_part, force_part = potential_field_values(
        atom_charges,
        cosine_phase_values,
        sine_phase_values,
        local_wave_vectors,
        own_weight,
        structure_real,
        structure_imaginary,
    )
    potential, forces = packed_total((potential_part, force_part), "inner")
    return (attention, potential, forces)


def solution(mesh):
    torus = Mesh(mesh.devices.reshape(4, 32, mesh.shape["inner"]), ("seq_0", "seq_1", "inner"))
    return jax.shard_map(
        local,
        mesh=torus,
        in_specs=(
            P("inner", None, SEQ),
            P("inner", None, SEQ),
            P("inner", None, SEQ),
            P(None, SEQ),
            P(),
            P(SEQ, None),
            P(),
            P("inner", None),
        ),
        out_specs=(P("inner", None, SEQ), P(None, SEQ), P(None, SEQ)),
        check_vma=False,
    )
```

profile of v0, /device:TPU:1, one launch (start us, length us, event | category | flops | bytes accessed | tf_op | source)
XLA Modules:
  0.0 315.3 jit_solution(15572017930314309585)
XLA Ops:
  0.6 2.4 copy.35
  3.0 1.5 reshape.189
  4.6 1.6 constant_dynamic-update-slice_fusion
  7.1 5.1 %collective-permute-start = (bf16[1,416,512]{2,1,0:T(8,128)(2,1)}, bf16[1,416,512]{2,1,0:T(8,128)(2,1)}, u32[]{:S(2)}, u32[]{:S(2)}) collective-permute-start(bf16[1,416,512]{2,1,0:T(8,128)(2,1)} %get-tuple-element.118), channel_id=1, source_target_pairs={{0,8},{8,16},{16,24},{24,32},{32,40},{40,48},{48,56},{56,64},{64,7... | collective-permute-start | bytes 1277960 | tf_op jit(solution)/shard_map/ppermute | solution.py:26
  12.3 1.3 collective-permute-start.1
  13.9 3.0 collective-permute-done
  16.9 4.6 %collective-permute-done.1 = bf16[1,416,512]{2,1,0:T(8,128)(2,1)} collective-permute-done((bf16[1,416,512]{2,1,0:T(8,128)(2,1)}, bf16[1,416,512]{2,1,0:T(8,128)(2,1)}, u32[]{:S(2)}, u32[]{:S(2)}) %collective-permute-start.1) | collective-permute-done | bytes 426016 | tf_op jit(solution)/shard_map/ppermute | solution.py:28
  21.4 1.4 pad_maximum_fusion
  22.8 1.7 copy.53
  24.5 50.3 %while.11 = (s32[]{:T(128)}, bf16[8,1,400,256]{3,2,1,0:T(8,128)(2,1)S(1)}, s32[8]{0:T(128)S(1)}, s32[8,3]{1,0:T(8,128)S(1)}, bf16[1,416,12,256]{3,1,2,0:T(8,128)...) while((s32[]{:T(128)}, bf16[8,1,400,256]{3,2,1,0:T(8,128)(2,1)S(1)}, ...), condition=%wide.region_3.4_spmd.clone, body=%wide.region_0.3_spmd.clone.sunk | while | flops 165585440 | bytes 7411955 | solution.py:193
  24.5 2.3 gather_fusion
  30.8 2.3 gather_fusion
  37.1 2.3 gather_fusion
  43.4 2.3 gather_fusion
  49.7 2.3 gather_fusion
  55.9 2.3 gather_fusion
  62.2 2.3 gather_fusion
  68.5 2.3 gather_fusion
  74.8 1.8 copy.38
  76.5 2.7 reshape.192
  80.6 16.0 %all-to-all-start = ((f32[8,16,2048]{2,1,0:T(8,128)}), f32[8,16,2048]{2,1,0:T(8,128)S(1)}, u32[]{:S(2)}, u32[]{:S(2)}) async-start(f32[8,16,2048]{2,1,0:T(8,128)} %broadcast_in_dim.78), calls=%async_computation | async-start | bytes 2097152 | tf_op jit(solution)/shard_map/all_to_all | solution.py:37
  96.9 14.5 %all-to-all-done = f32[8,16,2048]{2,1,0:T(8,128)S(1)} async-done(((f32[8,16,2048]{2,1,0:T(8,128)}), f32[8,16,2048]{2,1,0:T(8,128)S(1)}, u32[]{:S(2)}, u32[]{:S(2)}) %all-to-all-start) | async-done | bytes 1048608 | tf_op jit(solution)/shard_map/all_to_all | solution.py:37
  111.5 8.8 %fusion.24 = f32[16,256]{1,0:T(8,128)S(1)} fusion(f32[16,2048]{1,0:T(8,128)S(1)} %reduce_sum.45, f32[2048]{0:T(1024)S(1)} %bitcast.98, f32[256]{0:T(256)S(1)} %bitcast.114, f32[2048]{0:T(1024)S(1)} %bitcast.102, f32[256]{0:T(256)S(1)} %bitcast.110, f32[2048]{0:T(1024)S(1)} %bitcast.94, f32[256]{0:T(256)S(1)} %bitcast.106), kind=kOutput, calls=%fused_computation.39 | convolution fusion | flops 103813120 | bytes 175104 | tf_op jit(solution)/shard_map/dot_general | solution.py:97
  120.2 21.5 %fusion.27 = f32[16,256]{1,0:T(8,128)S(1)} fusion(f32[16,2048]{1,0:T(8,128)S(1)} %reduce_sum.45, f32[2048]{0:T(1024)S(1)} %bitcast.99, f32[256]{0:T(256)S(1)} %bitcast.115, f32[2048]{0:T(1024)S(1)} %bitcast.103, f32[256]{0:T(256)S(1)} %bitcast.111, f32[2048]{0:T(1024)S(1)} %bitcast.95, f32[256]{0:T(256)S(1)} %bitcast.107), kind=kOutput, calls=%fused_computation.40 | convolution fusion | flops 103813120 | bytes 175104 | tf_op jit(solution)/shard_map/dot_general | solution.py:97
  141.7 19.5 %all-reduce.2 = (f32[16,256]{1,0:T(8,128)S(1)}, f32[16,256]{1,0:T(8,128)S(1)}) all-reduce(f32[16,256]{1,0:T(8,128)S(1)} %fusion.24, f32[16,256]{1,0:T(8,128)S(1)} %fusion.27), channel_id=1, replica_groups=mesh['seq_0'=4,'seq_1'=32,'inner'=8] {'seq_0'}, use_global_device_ids=true, to_apply=%region_8.9 | all-reduce | flops 8192 | bytes 65536 | tf_op jit(solution)/shard_map/psum | solution.py:48
  161.2 79.9 %all-reduce.1 = (f32[16,256]{1,0:T(8,128)S(1)}, f32[16,256]{1,0:T(8,128)S(1)}) all-reduce(f32[16,256]{1,0:T(8,128)S(1)} %get-tuple-element.114, f32[16,256]{1,0:T(8,128)S(1)} %get-tuple-element.115), channel_id=1, replica_groups=mesh['seq_0'=4,'seq_1'=32,'inner'=8] {'seq_1'}, use_global_device_ids=true, to_apply=%region_9.10 | all-reduce | flops 8192 | bytes 65536 | tf_op jit(solution)/shard_map/psum | solution.py:48
  241.1 8.6 %fusion.17 = f32[64,2048]{1,0:T(8,128)S(1)} fusion(f32[2048]{0:T(1024)S(1)} %bitcast.100, f32[256]{0:T(256)S(1)} %bitcast.116, f32[2048]{0:T(1024)S(1)} %bitcast.104, f32[256]{0:T(256)S(1)} %bitcast.112, f32[2048]{0:T(1024)S(1)} %bitcast.96, f32[256]{0:T(256)S(1)} %bitcast.108, f32[48,256]{1,0:T(8,128)S(1)} %bitcast.93, f32[16,256]{1,0:T(8,128)S(1)} %get-tuple-element.128), kind=kOutput, calls=%fused_computation.36 | convolution fusion | flops 405815296 | bytes 617472 | tf_op jit(solution)/shard_map/dot_general | solution.py:137
  249.7 8.8 %convolution_add_fusion = f32[64,2048]{1,0:T(8,128)S(1)} fusion(f32[64,2048]{1,0:T(8,128)S(1)} %fusion.17, f32[2048]{0:T(1024)S(1)} %bitcast.101, f32[256]{0:T(256)S(1)} %bitcast.117, f32[2048]{0:T(1024)S(1)} %bitcast.105, f32[256]{0:T(256)S(1)} %bitcast.113, f32[2048]{0:T(1024)S(1)} %bitcast.97, f32[256]{0:T(256)S(1)} %bitcast.109, ...), kind=kOutput, calls=%fused_computation.31 | convolution fusion | flops 405946368 | bytes 1141760 | tf_op jit(solution)/shard_map/dot_general | solution.py:142
  258.8 1.7 broadcast_in_dim.79
  260.4 35.1 %all-to-all-start.1 = ((f32[8,1,38912]{2,1,0:T(1,128)}), f32[8,1,38912]{2,1,0:T(1,128)S(1)}, u32[]{:S(2)}, u32[]{:S(2)}) async-start(f32[8,1,38912]{2,1,0:T(1,128)} %broadcast_in_dim.79), calls=%async_computation.1 | async-start | bytes 2490368 | tf_op jit(solution)/shard_map/all_to_all | solution.py:37
  295.6 2.1 copy.40
  297.7 15.1 %all-to-all-done.1 = f32[8,1,38912]{2,1,0:T(1,128)S(1)} async-done(((f32[8,1,38912]{2,1,0:T(1,128)}), f32[8,1,38912]{2,1,0:T(1,128)S(1)}, u32[]{:S(2)}, u32[]{:S(2)}) %all-to-all-start.1) | async-done | bytes 1245216 | tf_op jit(solution)/shard_map/all_to_all | solution.py:37
  (175 shorter events, 36.6 us)
Async XLA Ops:
  0.6 78.7 %copy-start = (bf16[16,16]{1,0:T(8,128)(2,1)S(1)}, bf16[16,16]{1,0:T(8,128)(2,1)}, u32[]{:S(2)}) copy-start(bf16[16,16]{1,0:T(8,128)(2,1)} %param.17) | copy-start | bytes 1540
  3.0 1.5 copy-start.2
  4.5 9.0 %copy-start.3 = (bf16[1,16,2048]{2,1,0:T(8,128)(2,1)S(1)}, bf16[1,16,2048]{2,1,0:T(8,128)(2,1)}, u32[]{:S(2)}) copy-start(bf16[1,16,2048]{2,1,0:T(8,128)(2,1)} %param.10) | copy-start | bytes 196612
  4.6 9.1 %copy-start.6 = (s32[8,3]{0,1:T(4,128)S(1)}, s32[8,3]{0,1:T(4,128)}, u32[]{:S(2)}) copy-start(s32[8,3]{0,1:T(4,128)} %param.15) | copy-start | bytes 292
  4.6 9.1 %copy-start.5 = (s32[1024]{0:T(1024)S(1)}, s32[1024]{0:T(1024)}, u32[]{:S(2)}) copy-start(s32[1024]{0:T(1024)} %param.14) | copy-start | bytes 12292
  7.1 9.7 %collective-permute-start = (bf16[1,416,512]{2,1,0:T(8,128)(2,1)}, bf16[1,416,512]{2,1,0:T(8,128)(2,1)}, u32[]{:S(2)}, u32[]{:S(2)}) collective-permute-start(bf16[1,416,512]{2,1,0:T(8,128)(2,1)} %get-tuple-element.118), channel_id=1, source_target_pairs={{0,8},{8,16},{16,24},{24,32},{32,40},{40,48},{48,56},{56,64},{64,7... | collective-permute-start | bytes 1277960 | tf_op jit(solution)/shard_map/ppermute | solution.py:26
  12.3 9.2 %collective-permute-start.1 = (bf16[1,416,512]{2,1,0:T(8,128)(2,1)}, bf16[1,416,512]{2,1,0:T(8,128)(2,1)}, u32[]{:S(2)}, u32[]{:S(2)}) collective-permute-start(bf16[1,416,512]{2,1,0:T(8,128)(2,1)} %get-tuple-element.119), channel_id=1, source_target_pairs={{8,0},{16,8},{24,16},{32,24},{40,32},{48,40},{56,48},{64,56},{72,6... | collective-permute-start | bytes 1277960 | tf_op jit(solution)/shard_map/ppermute | solution.py:28
  79.2 17.4 %copy-start.1 = (s32[3,2048]{1,0:T(4,128)S(1)}, s32[3,2048]{1,0:T(4,128)}, u32[]{:S(2)}) copy-start(s32[3,2048]{1,0:T(4,128)} %param.16) | copy-start | bytes 73732
  79.2 17.7 %copy-start.4 = (f32[3,2048]{1,0:T(4,128)S(1)}, f32[3,2048]{1,0:T(4,128)}, u32[]{:S(2)}) copy-start(f32[3,2048]{1,0:T(4,128)} %param.13) | copy-start | bytes 73732
  80.6 30.8 %all-to-all-start = ((f32[8,16,2048]{2,1,0:T(8,128)}), f32[8,16,2048]{2,1,0:T(8,128)S(1)}, u32[]{:S(2)}, u32[]{:S(2)}) async-start(f32[8,16,2048]{2,1,0:T(8,128)} %broadcast_in_dim.78), calls=%async_computation | async-start | bytes 2097152 | tf_op jit(solution)/shard_map/all_to_all | solution.py:37
  260.4 52.4 %all-to-all-start.1 = ((f32[8,1,38912]{2,1,0:T(1,128)}), f32[8,1,38912]{2,1,0:T(1,128)S(1)}, u32[]{:S(2)}, u32[]{:S(2)}) async-start(f32[8,1,38912]{2,1,0:T(1,128)} %broadcast_in_dim.79), calls=%async_computation.1 | async-start | bytes 2490368 | tf_op jit(solution)/shard_map/all_to_all | solution.py:37
where the time goes:
time: 320 us; the launch traced here: 315 us
  blocking collectives  99.4 us (31%)
  starting transfers between devices  57.6 us (18%)
  matrix products  56.9 us (18%)
  local copies, waits for them, and re-layouts  50.1 us (16%)
  waiting for transfers between devices  37.2 us (12%)
  other arithmetic  12.4 us (4%)
    psum x2, blocking collectives, over_axes(): value = lax.psum(value, axis)  99.4 us
    all_to_all x2, starting transfers between devices, sent_to_all(): lax.all_to_all(jnp.broadcast_to(value[None], (length, *value.shape)), axi...  51.2 us
    dot_general x2, matrix products, contract(): lax.dot_general(atom_charges, wave_table, (((1,), (1,)), ((), ())), preci...  30.2 us
    all_to_all x2, waiting for transfers between devices, sent_to_all(): lax.all_to_all(jnp.broadcast_to(value[None], (length, *value.shape)), axi...  29.6 us
    gather x16, local copies, waits for them, and re-layouts, one_block(): jnp.take(banded, listed, axis=2).reshape(heads_here, row_width, NNB * BS)  20.7 us
    dot_general x1, matrix products, potential_field_values(): jnp.dot(sine_product, sine_phase_values, precision=lax.Precision.HIGHEST,...  8.83 us
    dot_general x1, matrix products, potential_field_values(): jnp.dot(cosine_product, cosine_phase_values, precision=lax.Precision.HIGH...  8.57 us
  transfers between devices with their start and end apart: 4, of which 4 were waited for; matrix products, arithmetic and copies ran while one was open for 1% of the time, Pallas kernels for 0%

commit v1 on v0

v1 whole, which is shorter than its diff:
```python
import jax
import jax.numpy as jnp
from jax import lax
from jax.experimental import pallas as pl
from jax.experimental.pallas import tpu as pltpu
from jax.sharding import Mesh
from jax.sharding import PartitionSpec as P

BS = 256
NNB = 3
NY, NZ, NX, NC = 4, 32, 4, 2
SEQ = ("y", "z")
INNER = ("x", "c")
NI = NX * NC
NSEQ = NY * NZ
GZ = 2
NG = NY * GZ
NR = NZ // GZ
NB = 8
F32, BF16 = jnp.float32, jnp.bfloat16
MESH = pl.DeviceIdType.MESH
DEAD = -1e30

ewald_scale = 40.0
ewald_damp = 0.02

COS = (1.0, -19.739208221435547, 64.93939208984375, -85.45665740966797, 60.242130279541016, -26.4046688079834, 7.800131320953369, -1.4531123638153076)
SIN = (6.2831854820251465, -41.34170150756836, 81.6052474975586, -76.70575714111328, 42.057369232177734, -15.084554672241211, 3.7759575843811035, -0.6150599718093872)


def poly(coeffs, u):
    y = jnp.full_like(u, coeffs[-1])
    for k in coeffs[-2::-1]:
        y = y * u + k
    return y


def cos_sin_turns(t):
    r = t - jnp.floor(t + 0.5)
    u = r * r
    return poly(COS, u), poly(SIN, u) * r


def nt(a, b):
    return lax.dot_general(a, b, (((1,), (1,)), ((), ())), preferred_element_type=F32)


def tn(a, b):
    return lax.dot_general(a, b, (((0,), (0,)), ((), ())), preferred_element_type=F32)


def nn(a, b):
    return jnp.dot(a, b, preferred_element_type=F32)


def kernel(
    q, k, frac, counts, nbr, iwv, cw, v_hbm,
    o_att, o_pot, o_for,
    v_own, v2, ks, qs, ps, rden, ob, v0f, a0, cwa, chg, xt, bt, wt, gs, rs, os_, gt, hs,
    sem_v, sem_o, halo_s, halo_r, a_s, a_r, c_s, c_r, r_s, r_r, f_s, f_r, t_s, t_r, g_s, g_r,
):
    y, z, x, c = (lax.axis_index(a) for a in ("y", "z", "x", "c"))
    inner = x * NC + c
    seq = y * NZ + z
    gid = y * GZ + lax.rem(z, GZ)
    rid = z // GZ
    first = seq * NB

    def at_seq(s):
        return {"y": s // NZ, "z": lax.rem(s, NZ)}

    def listed_at(g, j):
        return jnp.clip(nbr[g, j] - (first - 2), 0, NB + 3)

    right = at_seq(lax.rem(seq + 1, NSEQ))
    left = at_seq(lax.rem(seq + NSEQ - 1, NSEQ))

    def inner_peer(o):
        p = lax.rem(inner + o, NI)
        return p, {"x": p // NC, "c": lax.rem(p, NC)}

    def group_peer(o):
        p = lax.rem(gid + o, NG)
        return p, {"y": p // GZ, "z": rid * GZ + lax.rem(p, GZ)}

    def ring_peer(o):
        p = lax.rem(rid + o, NR)
        return p, {"z": p * GZ + lax.rem(z, GZ)}

    barrier = pltpu.get_barrier_semaphore()
    peers = [left, right]
    peers += [inner_peer(o)[1] for o in range(1, NI)]
    peers += [group_peer(o)[1] for o in range(1, NG)]
    peers += [ring_peer(o)[1] for o in range(1, NR)]
    for p in peers:
        pl.semaphore_signal(barrier, inc=1, device_id=p, device_id_type=MESH)

    load_v = pltpu.make_async_copy(v_hbm, v_own, sem_v)
    load_v.start()

    row16 = lax.broadcasted_iota(jnp.int32, (16, BS), 0)
    lane16 = lax.broadcasted_iota(jnp.int32, (16, BS), 1)
    for b in range(NB):
        cols = pl.ds(b * BS, BS)
        live = lane16 < counts[first + b]
        bias = jnp.where((row16 == 0) & jnp.logical_not(live), DEAD, 0.0)
        ks[b + 2, 0:16, :] = k[0, :, cols]
        ks[b + 2, 16:32, :] = bias.astype(BF16)
        qs[b, 0:16, :] = (q[0, :, cols].astype(F32) * 0.25).astype(BF16)
        qs[b, 16:32, :] = jnp.where(row16 == 0, 1.0, 0.0).astype(BF16)
    cwa[inner] = cw[...]

    load_v.wait()
    for ch in range(16):
        v0f[ch : ch + 1, :] = v_own[ch, 0:1, :].astype(F32)
    for b in range(NB):
        ks[b + 2, 32:48, :] = v0f[:, b * BS : (b + 1) * BS].astype(BF16)

    def send(src, dst, ssem, rsem, dev):
        cp = pltpu.make_async_remote_copy(
            src_ref=src, dst_ref=dst, send_sem=ssem, recv_sem=rsem, device_id=dev, device_id_type=MESH
        )
        cp.start()
        return cp

    pl.semaphore_wait(barrier, len(peers))
    kh = [
        send(ks.at[pl.ds(8, 2)], ks.at[pl.ds(0, 2)], halo_s.at[0], halo_r.at[0], right),
        send(ks.at[pl.ds(2, 2)], ks.at[pl.ds(10, 2)], halo_s.at[1], halo_r.at[1], left),
    ]
    cws = [
        send(cwa.at[inner], cwa.at[inner], c_s.at[o - 1], c_r.at[o - 1], inner_peer(o)[1])
        for o in range(1, NI)
    ]

    @pl.loop(0, NB)
    def _(b):
        for ch in range(16):
            v2[b + 2, ch, 0:25, :] = v_own[ch, :, pl.ds(pl.multiple_of(b * BS, BS), BS)]

    vh = [
        send(v2.at[pl.ds(8, 2)], v2.at[pl.ds(0, 2)], halo_s.at[2], halo_r.at[2], right),
        send(v2.at[pl.ds(2, 2)], v2.at[pl.ds(10, 2)], halo_s.at[3], halo_r.at[3], left),
    ]
    for cp in kh:
        cp.wait_recv()

    @pl.loop(0, NB)
    def _(g):
        listed = [listed_at(g, j) for j in range(NNB)]
        qa = qs[g]
        s = [tn(ks[i, 0:32, :], qa) for i in listed]
        m = s[0].max(axis=0, keepdims=True)
        for t in s[1:]:
            m = jnp.maximum(m, t.max(axis=0, keepdims=True))
        den = jnp.zeros((1, BS), F32)
        acc = jnp.zeros((16, BS), F32)
        for j, i in enumerate(listed):
            w = jnp.exp(s[j] - m)
            den += w.sum(axis=0, keepdims=True)
            wb = w.astype(BF16)
            ps[g, j] = wb
            acc += nn(ks[i, 32:48, :], wb)
        live_q = lax.broadcasted_iota(jnp.int32, (1, BS), 1) < counts[first + g]
        rd = jnp.where(live_q, 1.0 / den, 0.0)
        rden[g] = rd
        a0[inner, :, pl.ds(pl.multiple_of(g * BS, BS), BS)] = (acc * rd).astype(BF16)

    asend = [
        send(a0.at[inner], a0.at[inner], a_s.at[o - 1], a_r.at[o - 1], inner_peer(o)[1])
        for o in range(1, NI)
    ]

    n_atoms = NB * BS
    iota8 = lax.broadcasted_iota(jnp.int32, (8, n_atoms), 0).astype(F32)
    xc, xs = cos_sin_turns(frac[0:1, :] * iota8)
    xt[0] = xc
    xt[1] = xs
    u_tab = cos_sin_turns(frac[1:2, :] * iota8)
    v_tab = cos_sin_turns(frac[2:3, :] * iota8)
    for u in range(2):
        for v in range(2):
            for n in range(0, 8, 2):
                lo = u_tab[u][n : n + 1, :] * v_tab[v]
                hi = u_tab[u][n + 1 : n + 2, :] * v_tab[v]
                at = u * 128 + v * 64 + n * 8
                bt[at : at + 16, :] = jnp.concatenate([lo, hi], axis=0).astype(BF16)

    n0, n1, n2 = iwv[0:1, :], iwv[1:2, :], iwv[2:3, :]
    n_waves = iwv.shape[1]
    flip = n0 < 0
    n1 = jnp.where(flip, -n1, n1)
    n2 = jnp.where(flip, -n2, n2)
    s1 = jnp.where(n1 < 0, -1.0, 1.0)
    s2 = jnp.where(n2 < 0, -1.0, 1.0)
    place = jnp.abs(n1) * 8 + jnp.abs(n2)
    rows128 = lax.broadcasted_iota(jnp.int32, (128, n_waves), 0)
    hot = jnp.where((rows128 & 63) == place, 1.0, 0.0).astype(BF16)
    mine = lax.broadcasted_iota(jnp.int32, (8, n_waves), 0) == jnp.abs(n0)
    coeffs = [jnp.ones_like(s1), s1, s2, s1 * s2]
    listed = jnp.concatenate([jnp.where(mine, cf, 0.0) for cf in coeffs], axis=0).astype(BF16)
    cnt = nt(listed, hot)
    d_row = lax.broadcasted_iota(jnp.int32, (8, 128), 0)
    l_row = lax.broadcasted_iota(jnp.int32, (8, 128), 1)
    b_row = (l_row & 63) >> 3
    g_row = l_row & 7
    norm2 = jnp.maximum(d_row * d_row + b_row * b_row + g_row * g_row, 1).astype(F32)
    kw = ewald_scale * jnp.exp(-ewald_damp * norm2) / norm2
    for t in range(4):
        wt[t] = cnt[t * 8 : (t + 1) * 8] * kw

    for cp in cws + asend:
        cp.wait_recv()
    charges = tn(cwa[...].reshape(NI * 16, 16), a0[...].reshape(NI * 16, n_atoms))
    chg[...] = charges

    own_c = xt[0, pl.ds(inner, 1), :]
    own_s = xt[1, pl.ds(inner, 1), :]
    amp = jnp.concatenate([charges * own_c, charges * own_s], axis=0) * (1.0 / 512.0)
    amp_h = amp.astype(BF16)
    amp_l = (amp - amp_h.astype(F32)).astype(BF16)
    both = nt(jnp.concatenate([amp_h, amp_l], axis=0), bt[...])
    part = both[0:32] + both[32:64]
    for p in range(8):
        gs[p] = part[(p // 2) * 8 : (p // 2) * 8 + 8, (p % 2) * 128 : (p % 2) * 128 + 128]

    rsend = []
    for o in range(1, NG):
        p, dev = group_peer(o)
        rsend.append(send(gs.at[p], rs.at[gid], r_s.at[o - 1], r_r.at[o - 1], dev))
    rs[gid] = gs[gid]
    for cp in rsend:
        cp.wait_recv()
    os_[rid] = jnp.sum(rs[...], axis=0)
    fsend = [
        send(os_.at[rid], os_.at[rid], f_s.at[o - 1], f_r.at[o - 1], ring_peer(o)[1])
        for o in range(1, NR)
    ]

    for cp in vh:
        cp.wait_recv()

    @pl.loop(0, NB)
    def _(g):
        acc = jnp.zeros((512, BS), F32)
        for j in range(NNB):
            i = listed_at(g, j)
            acc += nn(v2[i].reshape(512, BS), ps[g, j])
        ob[g] = (acc * rden[g]).astype(BF16).reshape(16, 32, BS)

    outs = []
    for g in range(NB):
        cp = pltpu.make_async_copy(ob.at[g], o_att.at[:, :, pl.ds(g * BS, BS)], sem_o.at[g])
        cp.start()
        outs.append(cp)

    for cp in fsend:
        cp.wait_recv()
    gt[inner, gid] = jnp.sum(os_[...], axis=0)
    tsend = [
        send(gt.at[inner, gid], gt.at[inner, gid], t_s.at[o - 1], t_r.at[o - 1], group_peer(o)[1])
        for o in range(1, NG)
    ]
    for cp in tsend:
        cp.wait_recv()
    gsend = [
        send(gt.at[inner], gt.at[inner], g_s.at[o - 1], g_r.at[o - 1], inner_peer(o)[1])
        for o in range(1, NI)
    ]
    for cp in gsend:
        cp.wait_recv()

    lane = lax.broadcasted_iota(jnp.int32, (1, 128), 1)
    sgn = jnp.where(lane < 64, -1.0, 1.0)
    w_n1 = ((lane & 63) >> 3).astype(F32)
    w_n2 = (lane & 7).astype(F32)

    def swap(a):
        return pltpu.roll(a, 64, 1)

    for d in range(NI):
        w0, w1, w2, w12 = (wt[t, d : d + 1, :] for t in range(4))
        g4 = {
            (p, u): jnp.concatenate([gt[d, 4 * p + u], gt[d, 4 * p + 2 + u]], axis=0)
            for p in range(2)
            for u in range(2)
        }
        h = {}
        for p in range(2):
            for u in range(2):
                su = sgn if u == 0 else -sgn
                sp = sgn if p == 0 else -sgn
                pu = -1.0 if p == u else 1.0
                h[p, u] = (
                    w0 * g4[p, u]
                    + (su * w12) * swap(g4[p, 1 - u])
                    + (pu * w1) * g4[1 - p, 1 - u]
                    + (sp * w2) * swap(g4[1 - p, u])
                )
        for p in range(2):
            r = p * 16
            hs[d, r : r + 16, 0:128] = h[p, 0].astype(BF16)
            hs[d, r : r + 16, 128:256] = h[p, 1].astype(BF16)
            hs[d, 32 + r : 48 + r, 0:128] = (-w_n1 * h[p, 1]).astype(BF16)
            hs[d, 32 + r : 48 + r, 128:256] = (w_n1 * h[p, 0]).astype(BF16)
            for u in range(2):
                hs[d, 64 + r : 80 + r, u * 128 : u * 128 + 128] = (
                    (w_n2 * sgn) * swap(h[p, u])
                ).astype(BF16)

    @pl.loop(0, NB)
    def _(t):
        cols = pl.ds(pl.multiple_of(t * BS, BS), BS)
        basis = bt[:, cols]
        pot = jnp.zeros((16, BS), F32)
        fx = jnp.zeros((16, BS), F32)
        fy = jnp.zeros((16, BS), F32)
        fz = jnp.zeros((16, BS), F32)
        for d in range(NI):
            r = nn(hs[d], basis)
            xc = xt[0, d : d + 1, cols]
            xs = xt[1, d : d + 1, cols]
            pot += xc * r[0:16] + xs * r[16:32]
            if d:
                fx += (d * xs) * r[0:16] - (d * xc) * r[16:32]
            fy += xc * r[32:48] + xs * r[48:64]
            fz += xc * r[64:80] + xs * r[80:96]
        o_pot[:, cols] = pot
        ch = chg[:, cols]
        for i, f in enumerate((fx, fy, fz)):
            o_for[i : i + 1, cols] = jnp.sum(ch * f, axis=0, keepdims=True)

    for cp in outs:
        cp.wait()
    for cp in kh + cws + vh + asend + rsend + fsend + tsend + gsend:
        cp.wait_send()


def local(queries, key_states, value_states, fractional, block_counts, neighbors, integer_wave_vectors, charge_weight):
    n_atoms = queries.shape[2]
    vmem = pl.BlockSpec(memory_space=pltpu.VMEM)
    smem = pl.BlockSpec(memory_space=pltpu.SMEM)
    hbm = pl.BlockSpec(memory_space=pl.ANY)
    dma = pltpu.SemaphoreType.DMA
    attention, potential, forces = pl.pallas_call(
        kernel,
        out_shape=(
            jax.ShapeDtypeStruct((16, 32, n_atoms), BF16),
            jax.ShapeDtypeStruct((16, n_atoms), F32),
            jax.ShapeDtypeStruct((3, n_atoms), F32),
        ),
        in_specs=[vmem, vmem, vmem, smem, smem, vmem, vmem, hbm],
        out_specs=(hbm, vmem, vmem),
        scratch_shapes=[
            pltpu.VMEM((16, 25, n_atoms), BF16),
            pltpu.VMEM((NB + 4, 16, 32, BS), BF16),
            pltpu.VMEM((NB + 4, 48, BS), BF16),
            pltpu.VMEM((NB, 32, BS), BF16),
            pltpu.VMEM((NB, NNB, BS, BS), BF16),
            pltpu.VMEM((NB, 1, BS), F32),
            pltpu.VMEM((NB, 16, 32, BS), BF16),
            pltpu.VMEM((16, n_atoms), F32),
            pltpu.VMEM((NI, 16, n_atoms), BF16),
            pltpu.VMEM((NI, 16, 16), BF16),
            pltpu.VMEM((16, n_atoms), F32),
            pltpu.VMEM((2, 8, n_atoms), F32),
            pltpu.VMEM((256, n_atoms), BF16),
            pltpu.VMEM((4, 8, 128), F32),
            pltpu.VMEM((NG, 8, 128), F32),
            pltpu.VMEM((NG, 8, 128), F32),
            pltpu.VMEM((NR, 8, 128), F32),
            pltpu.VMEM((NI, NG, 8, 128), F32),
            pltpu.VMEM((NI, 96, 256), BF16),
            dma,
            dma((NB,)),
            dma((4,)),
            dma((4,)),
            dma((NI - 1,)),
            dma((NI - 1,)),
            dma((NI - 1,)),
            dma((NI - 1,)),
            dma((NG - 1,)),
            dma((NG - 1,)),
            dma((NR - 1,)),
            dma((NR - 1,)),
            dma((NG - 1,)),
            dma((NG - 1,)),
            dma((NI - 1,)),
            dma((NI - 1,)),
        ],
        compiler_params=pltpu.CompilerParams(
            collective_id=0, has_side_effects=True, vmem_limit_bytes=40 << 20
        ),
    )(queries, key_states, fractional, block_counts, neighbors, integer_wave_vectors, charge_weight, value_states)
    return attention[:, :25, :], potential, forces


def solution(mesh):
    torus = Mesh(mesh.devices.reshape(NY, NZ, NX, NC), ("y", "z", "x", "c"))
    return jax.shard_map(
        local,
        mesh=torus,
        in_specs=(
            P(INNER, None, SEQ),
            P(INNER, None, SEQ),
            P(INNER, None, SEQ),
            P(None, SEQ),
            P(),
            P(SEQ, None),
            P(),
            P(INNER, None),
        ),
        out_specs=(P(INNER, None, SEQ), P(None, SEQ), P(None, SEQ)),
        check_vma=False,
    )
```

time: 320 us -> 82.2 us (0.26); the launches traced: 315 us -> 82 us
  blocking collectives: 99.4 us -> 0 us
  Pallas kernels: 0 us -> 74.6 us
  starting transfers between devices: 57.6 us -> 0 us
  matrix products: 56.9 us -> 0 us
  local copies, waits for them, and re-layouts: 50.1 us -> 6.57 us
  waiting for transfers between devices: 37.2 us -> 0 us
  other arithmetic: 12.4 us -> 0 us
    psum x2 -> x0, blocking collectives: 99.4 us -> none  [over_axes(): value = lax.psum(value, axis)]
    pallas_call x0 -> x1, Pallas kernels: none -> 74.6 us  [local(): pl.pallas_call(kernel, out_shape=(jax.ShapeDtypeStruct((16, 32, n_atoms),...]
    dot_general x21 -> x0, matrix products: 56.9 us -> none  [the longest x2 30.2 us: contract(): lax.dot_general(atom_charges, wave_table, (((1,), (1,)), ((), ())), preci...]
    all_to_all x2 -> x0, starting transfers between devices: 51.2 us -> none  [sent_to_all(): lax.all_to_all(jnp.broadcast_to(value[None], (length, *value.shape)), axi...]
    all_to_all x2 -> x0, waiting for transfers between devices: 29.6 us -> none  [sent_to_all(): lax.all_to_all(jnp.broadcast_to(value[None], (length, *value.shape)), axi...]
    gather x32 -> x0, local copies, waits for them, and re-layouts: 25.3 us -> none  [the longest x16 20.7 us: one_block(): jnp.take(banded, listed, axis=2).reshape(heads_here, row_width, NNB * BS)]
    ppermute x2 -> x0, waiting for transfers between devices: 7.54 us -> none  [the longest x1 4.57 us: padded(): lax.ppermute(head, axis, [((i + 1) % count, i) for i in range(ends)])]
    ppermute x2 -> x0, starting transfers between devices: 6.41 us -> none  [the longest x1 5.13 us: padded(): lax.ppermute(tail, axis, [(i, (i + 1) % count) for i in range(ends)])]
  transfers between devices with their start and end apart: 4 -> 0, of which waited for: 4 -> 0; matrix products, arithmetic and copies ran while one was open for 1% -> 0% of each run, Pallas kernels for 0% -> 0%
where the time goes in v1:
time: 82.2 us; the launch traced here: 82 us
  Pallas kernels  74.6 us (91%)
  local copies, waits for them, and re-layouts  6.57 us (8%)
    pallas_call x1, Pallas kernels, local(): pl.pallas_call(kernel, out_shape=(jax.ShapeDtypeStruct((16, 32, n_atoms),...  74.6 us
    unnamed x17, local copies, waits for them, and re-layouts  6.57 us

profile of v1, /device:TPU:1, one launch (start us, length us, event | category | flops | bytes accessed | tf_op | source)
XLA Modules:
  0.0 82.0 jit_solution(17016722280011497045)
XLA Ops:
  0.6 0.0 copy-start.5
  0.6 0.0 copy-start.3
  0.7 0.0 copy-start.4
  0.7 0.0 copy-start.2
  0.7 0.0 copy-start.1
  0.7 0.0 copy-start
  0.7 0.8 copy.11.nbr
  1.5 2.4 %copy.12.v_hbm = bf16[16,25,2048]{2,1,0:T(8,128)(2,1)S(1)} copy(bf16[16,25,2048]{2,0,1:T(8,128)(2,1)} %param.10) | data formatting | bytes 3276800 | tf_op args[2]
  3.9 0.0 copy-done.5
  3.9 0.0 copy-done.3
  3.9 0.0 copy-done.4
  3.9 0.0 copy-done.2
  3.9 0.0 copy-done.1
  3.9 0.0 copy-done
  3.9 74.6 %shard_map.103 = (bf16[16,32,2048]{2,1,0:T(8,128)(2,1)S(1)}, f32[16,2048]{1,0:T(8,128)S(1)}, f32[3,2048]{1,0:T(4,128)S(1)}) custom-call(bf16[1,16,2048]{2,1,0:T(8,128)(2,1)S(1)} %copy-done, bf16[1,16,2048]{2,1,0:T(8,128)(2,1)S(1)} %copy-done.1, f32[3,2048]{1,0:T(4,128)S(1)} %copy-done.2, s32[1024]{0:T(1024)S(1)} %copy-done.4, s32[8,3]{1,0:T(8,128)S(1)} %copy.11.nbr, ...), custom_call_target="tpu_custom_call" | custom-call | tf_op jit(solution)/shard_map/pallas_call | solution.py:345
  78.6 2.1 %copy.13 = bf16[16,25,2048]{2,0,1:T(8,128)(2,1)} copy(bf16[16,25,2048]{2,1,0:T(8,128)(2,1)S(1)} %bitcast.1) | data formatting | bytes 3276800
  80.7 0.7 copy.16
  81.4 0.6 copy.17
Async XLA Ops:
  0.6 3.2 %copy-start.5 = (bf16[16,16]{1,0:T(8,128)(2,1)S(1)}, bf16[16,16]{1,0:T(8,128)(2,1)}, u32[]{:S(2)}) copy-start(bf16[16,16]{1,0:T(8,128)(2,1)} %cw.1) | copy-start | bytes 1540
  0.6 3.2 %copy-start.3 = (s32[3,2048]{1,0:T(4,128)S(1)}, s32[3,2048]{1,0:T(4,128)}, u32[]{:S(2)}) copy-start(s32[3,2048]{1,0:T(4,128)} %iwv.1) | copy-start | bytes 73732
  0.7 3.2 %copy-start.4 = (s32[1024]{0:T(1024)S(1)}, s32[1024]{0:T(1024)}, u32[]{:S(2)}) copy-start(s32[1024]{0:T(1024)} %counts.1) | copy-start | bytes 12292
  0.7 3.2 %copy-start.2 = (f32[3,2048]{1,0:T(4,128)S(1)}, f32[3,2048]{1,0:T(4,128)}, u32[]{:S(2)}) copy-start(f32[3,2048]{1,0:T(4,128)} %frac.1) | copy-start | bytes 73732
  0.7 3.2 %copy-start.1 = (bf16[1,16,2048]{2,1,0:T(8,128)(2,1)S(1)}, bf16[1,16,2048]{2,1,0:T(8,128)(2,1)}, u32[]{:S(2)}) copy-start(bf16[1,16,2048]{2,1,0:T(8,128)(2,1)} %k.1) | copy-start | bytes 196612
  0.7 3.2 %copy-start = (bf16[1,16,2048]{2,1,0:T(8,128)(2,1)S(1)}, bf16[1,16,2048]{2,1,0:T(8,128)(2,1)}, u32[]{:S(2)}) copy-start(bf16[1,16,2048]{2,1,0:T(8,128)(2,1)} %q.1) | copy-start | bytes 196612

commit v2 on v1

v2 whole, which is shorter than its diff:
```python
import jax
import jax.numpy as jnp
from jax import lax
from jax.experimental import pallas as pl
from jax.experimental.pallas import tpu as pltpu
from jax.sharding import Mesh
from jax.sharding import PartitionSpec as P

BS = 256
NNB = 3
NY, NZ, NX, NC = 4, 32, 4, 2
SEQ = ("y", "z")
INNER = ("x", "c")
NI = NX * NC
NSEQ = NY * NZ
GZ = 2
NG = NY * GZ
NR = NZ // GZ
NB = 8
F32, BF16 = jnp.float32, jnp.bfloat16
MESH = pl.DeviceIdType.MESH
DEAD = -1e30

ewald_scale = 40.0
ewald_damp = 0.02

COS = (1.0, -19.739208221435547, 64.93939208984375, -85.45665740966797, 60.242130279541016, -26.4046688079834, 7.800131320953369, -1.4531123638153076)
SIN = (6.2831854820251465, -41.34170150756836, 81.6052474975586, -76.70575714111328, 42.057369232177734, -15.084554672241211, 3.7759575843811035, -0.6150599718093872)


def poly(coeffs, u):
    y = jnp.full_like(u, coeffs[-1])
    for k in coeffs[-2::-1]:
        y = y * u + k
    return y


def cos_sin_turns(t):
    r = t - jnp.floor(t + 0.5)
    u = r * r
    return poly(COS, u), poly(SIN, u) * r


def nt(a, b):
    return lax.dot_general(a, b, (((1,), (1,)), ((), ())), preferred_element_type=F32)


def tn(a, b):
    return lax.dot_general(a, b, (((0,), (0,)), ((), ())), preferred_element_type=F32)


def nn(a, b):
    return jnp.dot(a, b, preferred_element_type=F32)


def listed_at(nbr, g, j, low, high):
    return jnp.clip(nbr[j, g] - low, 0, high)


def kernel(
    q_hbm, k_hbm, frac_hbm, counts_hbm, nbr_hbm, iwv_hbm, cw_hbm, v_hbm,
    att_hbm, gt_hbm, wt_hbm, xt_hbm, bt_hbm, chg_hbm,
    ob, gt, wt, xt, bt, chg, sem_o,
    q, k, frac, counts, nbr, iwv, cw, sem_i, v2, v0, ks, kin, kb, qs, ps, rden, a0, cwa, gs, rs, os_,
    sem_v, sem_v0, known, halo_s, halo_r, a_s, a_r, af_s, af_r, c_s, c_r, r_s, r_r, f_s, f_r, t_s, t_r, g_s, g_r, gf_s, gf_r,
):
    y, z, x, c = (lax.axis_index(a) for a in ("y", "z", "x", "c"))
    inner = x * NC + c
    seq = y * NZ + z
    gid = y * GZ + lax.rem(z, GZ)
    rid = z // GZ
    first = seq * NB

    def at_seq(s):
        return {"y": s // NZ, "z": lax.rem(s, NZ)}

    right = at_seq(lax.rem(seq + 1, NSEQ))
    left = at_seq(lax.rem(seq + NSEQ - 1, NSEQ))
    other = {"c": 1 - c}

    def inner_peer(o):
        p = lax.rem(inner + o, NI)
        return {"x": p // NC, "c": lax.rem(p, NC)}

    def x_peer(o):
        return {"x": lax.rem(x + o, NX)}

    def x_from(o):
        return lax.rem(x + NX - o, NX) * NC + c

    def group_peer(o):
        p = lax.rem(gid + o, NG)
        return p, {"y": p // GZ, "z": rid * GZ + lax.rem(p, GZ)}

    def ring_peer(o):
        p = lax.rem(rid + o, NR)
        return {"z": p * GZ + lax.rem(z, GZ)}

    pairs = ((k_hbm, k), (counts_hbm, counts), (q_hbm, q), (cw_hbm, cw), (nbr_hbm, nbr), (frac_hbm, frac), (iwv_hbm, iwv))
    takes = [pltpu.make_async_copy(a, b, sem_i.at[i]) for i, (a, b) in enumerate(pairs)]
    load_v0 = pltpu.make_async_copy(v_hbm.at[0], v0, sem_v0)
    for cp in takes[:2] + [load_v0] + takes[2:]:
        cp.start()

    barrier = pltpu.get_barrier_semaphore()
    near = [left, right, ring_peer(1), ring_peer(NR - 1)]
    near += [inner_peer(o) for o in range(1, NI)]
    near += [group_peer(o)[1] for o in range(1, NG)]
    for p in near:
        pl.semaphore_signal(barrier, inc=1, device_id=p, device_id_type=MESH)

    def tell(r):
        for o in (1 << r, NR - (1 << r)):
            pl.semaphore_signal(known.at[r], inc=1, device_id=ring_peer(o), device_id_type=MESH)

    def hear(r):
        pl.semaphore_wait(known.at[r], 2)

    loads = []
    for b in (0, 1, 6, 7, 2, 3, 4, 5):
        cp = pltpu.make_async_copy(v_hbm.at[:, :, pl.ds(b * BS, BS)], v2.at[b + 2], sem_v.at[b])
        cp.start()
        loads.append(cp)

    for cp in takes[:5]:
        cp.wait()

    row16 = lax.broadcasted_iota(jnp.int32, (16, BS), 0)
    lane16 = lax.broadcasted_iota(jnp.int32, (16, BS), 1)
    for b in range(NB):
        cols = pl.ds(b * BS, BS)
        live = lane16 < counts[first + b]
        bias = jnp.where((row16 == 0) & jnp.logical_not(live), DEAD, 0.0)
        ks[b, 0:16, :] = k[0, :, cols]
        ks[b, 16:32, :] = bias.astype(BF16)
        qs[b, 0:16, :] = (q[0, :, cols].astype(F32) * 0.25).astype(BF16)
        qs[b, 16:32, :] = jnp.where(row16 == 0, 1.0, 0.0).astype(BF16)
    cwa[inner] = cw[...]
    load_v0.wait()
    for b in range(NB):
        ks[b, 32:48, :] = v0[:, b * BS : (b + 1) * BS]

    def send(src, dst, ssem, rsem, dev):
        cp = pltpu.make_async_remote_copy(
            src_ref=src, dst_ref=dst, send_sem=ssem, recv_sem=rsem, device_id=dev, device_id_type=MESH
        )
        cp.start()
        return cp

    pl.semaphore_wait(barrier, len(near))
    kh = [
        send(ks.at[pl.ds(6, 2)], kin.at[pl.ds(0, 2)], halo_s.at[0], halo_r.at[0], right),
        send(ks.at[pl.ds(0, 2)], kin.at[pl.ds(2, 2)], halo_s.at[1], halo_r.at[1], left),
    ]
    tell(0)
    cws = [
        send(cwa.at[inner], cwa.at[inner], c_s.at[o - 1], c_r.at[o - 1], inner_peer(o))
        for o in range(1, NI)
    ]
    for cp in loads[:4]:
        cp.wait()
    vh = [
        send(v2.at[pl.ds(8, 2)], v2.at[pl.ds(0, 2)], halo_s.at[2], halo_r.at[2], right),
        send(v2.at[pl.ds(2, 2)], v2.at[pl.ds(10, 2)], halo_s.at[3], halo_r.at[3], left),
    ]

    def attend(src, low, high, at):
        g = lax.rem(at + 2, NB)
        listed = [listed_at(nbr, g, j, low, high) for j in range(NNB)]
        qa = qs[g]
        s = [tn(src[i, 0:32, :], qa) for i in listed]
        m = s[0].max(axis=0, keepdims=True)
        for t in s[1:]:
            m = jnp.maximum(m, t.max(axis=0, keepdims=True))
        den = jnp.zeros((1, BS), F32)
        acc = jnp.zeros((16, BS), F32)
        for j, i in enumerate(listed):
            w = jnp.exp(s[j] - m)
            den += w.sum(axis=0, keepdims=True)
            wb = w.astype(BF16)
            ps[g, j] = wb
            acc += nn(src[i, 32:48, :], wb)
        live_q = lax.broadcasted_iota(jnp.int32, (1, BS), 1) < counts[first + g]
        rd = jnp.where(live_q, 1.0 / den, 0.0)
        rden[g] = rd
        a0[inner, at] = (acc * rd).astype(BF16)

    def spread(half):
        mine = a0.at[inner, pl.ds(4 * half, 4)]
        out = [send(mine, mine, a_s.at[half, o - 1], a_r.at[half, o - 1], x_peer(o)) for o in range(1, NX)]
        return out, [send(mine, mine, af_s.at[half, 0], af_r.at[half, 0], other)]

    def pass_on(half, out, on):
        for o in range(1, NX):
            out[o - 1].wait_recv()
            got = a0.at[x_from(o), pl.ds(4 * half, 4)]
            on.append(send(got, got, af_s.at[half, o], af_r.at[half, o], other))

    @pl.loop(0, 4)
    def _(at):
        attend(ks, first, NB - 1, at)

    out0, on0 = spread(0)
    for cp in kh:
        cp.wait_recv()
    hear(0)
    tell(1)
    kb[0:2] = kin[0:2]
    kb[2:10] = ks[...]
    kb[10:12] = kin[2:4]

    @pl.loop(4, 8)
    def _(at):
        attend(kb, first - 2, NB + 3, at)

    out1, on1 = spread(1)
    pass_on(0, out0, on0)
    hear(1)
    tell(2)

    for cp in takes[5:]:
        cp.wait()

    n_atoms = NB * BS
    iota8 = lax.broadcasted_iota(jnp.int32, (8, n_atoms), 0).astype(F32)
    xc, xs = cos_sin_turns(frac[0:1, :] * iota8)
    xt[0] = xc
    xt[1] = xs
    u_tab = cos_sin_turns(frac[1:2, :] * iota8)
    v_tab = cos_sin_turns(frac[2:3, :] * iota8)
    for u in range(2):
        for v in range(2):
            for n in range(0, 8, 2):
                lo = u_tab[u][n : n + 1, :] * v_tab[v]
                hi = u_tab[u][n + 1 : n + 2, :] * v_tab[v]
                at = u * 128 + v * 64 + n * 8
                bt[at : at + 16, :] = jnp.concatenate([lo, hi], axis=0).astype(BF16)

    stored = []

    def store(i, src, dst):
        cp = pltpu.make_async_copy(src, dst, sem_o.at[i])
        cp.start()
        stored.append(cp)

    store(0, bt, bt_hbm)
    store(1, xt, xt_hbm)

    pass_on(1, out1, on1)
    for cp in cws + on0:
        cp.wait_recv()

    def charge(at):
        g = (at + 2) % NB
        r = tn(cwa[...].reshape(NI * 16, 16), a0[:, at].reshape(NI * 16, BS))
        chg[:, g * BS : (g + 1) * BS] = r

    for at in range(4):
        charge(at)
    for cp in on1:
        cp.wait_recv()
    for at in range(4, 8):
        charge(at)

    store(2, chg, chg_hbm)

    charges = chg[...]
    own_c = xt[0, pl.ds(inner, 1), :]
    own_s = xt[1, pl.ds(inner, 1), :]
    amp = jnp.concatenate([charges * own_c, charges * own_s], axis=0) * (1.0 / 512.0)
    amp_h = amp.astype(BF16)
    amp_l = (amp - amp_h.astype(F32)).astype(BF16)
    both = nt(jnp.concatenate([amp_h, amp_l], axis=0), bt[...])
    part = both[0:32] + both[32:64]
    for p in range(8):
        gs[p] = part[(p // 2) * 8 : (p // 2) * 8 + 8, (p % 2) * 128 : (p % 2) * 128 + 128]

    rsend = []
    for o in range(1, NG):
        p, dev = group_peer(o)
        rsend.append(send(gs.at[p], rs.at[gid], r_s.at[o - 1], r_r.at[o - 1], dev))
    rs[gid] = gs[gid]
    hear(2)
    for cp in rsend:
        cp.wait_recv()
    os_[rid] = jnp.sum(rs[...], axis=0)
    fsend = [
        send(os_.at[rid], os_.at[rid], f_s.at[o - 1], f_r.at[o - 1], ring_peer(o))
        for o in range(1, NR)
    ]

    n0, n1, n2 = iwv[0:1, :], iwv[1:2, :], iwv[2:3, :]
    n_waves = iwv.shape[1]
    flip = n0 < 0
    n1 = jnp.where(flip, -n1, n1)
    n2 = jnp.where(flip, -n2, n2)
    s1 = jnp.where(n1 < 0, -1.0, 1.0)
    s2 = jnp.where(n2 < 0, -1.0, 1.0)
    place = jnp.abs(n1) * 8 + jnp.abs(n2)
    rows128 = lax.broadcasted_iota(jnp.int32, (128, n_waves), 0)
    hot = jnp.where((rows128 & 63) == place, 1.0, 0.0).astype(BF16)
    mine = lax.broadcasted_iota(jnp.int32, (8, n_waves), 0) == jnp.abs(n0)
    coeffs = [jnp.ones_like(s1), s1, s2, s1 * s2]
    listed = jnp.concatenate([jnp.where(mine, cf, 0.0) for cf in coeffs], axis=0).astype(BF16)
    cnt = nt(listed, hot)
    d_row = lax.broadcasted_iota(jnp.int32, (8, 128), 0)
    l_row = lax.broadcasted_iota(jnp.int32, (8, 128), 1)
    b_row = (l_row & 63) >> 3
    g_row = l_row & 7
    norm2 = jnp.maximum(d_row * d_row + b_row * b_row + g_row * g_row, 1).astype(F32)
    kw = ewald_scale * jnp.exp(-ewald_damp * norm2) / norm2
    for t in range(4):
        wt[t] = cnt[t * 8 : (t + 1) * 8] * kw
    store(3, wt, wt_hbm)

    for cp in loads[4:]:
        cp.wait()
    for cp in vh:
        cp.wait_recv()

    @pl.loop(0, NB)
    def _(g):
        acc = jnp.zeros((400, BS), F32)
        for j in range(NNB):
            i = listed_at(nbr, g, j, first - 2, NB + 3)
            acc += nn(v2[i].reshape(400, BS), ps[g, j])
        ob[:, :, pl.ds(pl.multiple_of(g * BS, BS), BS)] = (acc * rden[g]).astype(BF16).reshape(25, 16, BS)

    store(4, ob, att_hbm)

    for cp in fsend:
        cp.wait_recv()
    gt[inner, gid] = jnp.sum(os_[...], axis=0)
    tsend = [
        send(gt.at[inner, gid], gt.at[inner, gid], t_s.at[o - 1], t_r.at[o - 1], group_peer(o)[1])
        for o in range(1, NG)
    ]
    for cp in tsend:
        cp.wait_recv()
    gsend = [send(gt.at[inner], gt.at[inner], g_s.at[o - 1], g_r.at[o - 1], x_peer(o)) for o in range(1, NX)]
    gon = [send(gt.at[inner], gt.at[inner], gf_s.at[0], gf_r.at[0], other)]
    for o in range(1, NX):
        gsend[o - 1].wait_recv()
        got = gt.at[x_from(o)]
        gon.append(send(got, got, gf_s.at[o], gf_r.at[o], other))
    for cp in gon:
        cp.wait_recv()
    store(5, gt, gt_hbm)
    for cp in kh + cws + vh + out0 + on0 + out1 + on1 + rsend + fsend + tsend + gsend + gon:
        cp.wait_send()
    for cp in stored:
        cp.wait()


def field(
    att_hbm, gt_hbm, wt_hbm, xt_hbm, bt_hbm, chg_hbm, o_att, o_pot, o_for, att, gt, wt, xt, bt, chg, hs, sem
):
    pairs = ((gt_hbm, gt), (wt_hbm, wt), (bt_hbm, bt), (xt_hbm, xt), (chg_hbm, chg), (att_hbm, att))
    takes = [pltpu.make_async_copy(a, b, sem.at[i]) for i, (a, b) in enumerate(pairs)]
    for cp in takes:
        cp.start()
    for cp in takes[:2]:
        cp.wait()

    lane = lax.broadcasted_iota(jnp.int32, (1, 128), 1)
    sgn = jnp.where(lane < 64, -1.0, 1.0)
    w_n1 = ((lane & 63) >> 3).astype(F32)
    w_n2 = (lane & 7).astype(F32)

    def swap(a):
        return pltpu.roll(a, 64, 1)

    for d in range(NI):
        w0, w1, w2, w12 = (wt[t, d : d + 1, :] for t in range(4))
        g4 = {
            (p, u): jnp.concatenate([gt[d, 4 * p + u], gt[d, 4 * p + 2 + u]], axis=0)
            for p in range(2)
            for u in range(2)
        }
        h = {}
        for p in range(2):
            for u in range(2):
                su = sgn if u == 0 else -sgn
                sp = sgn if p == 0 else -sgn
                pu = -1.0 if p == u else 1.0
                h[p, u] = (
                    w0 * g4[p, u]
                    + (su * w12) * swap(g4[p, 1 - u])
                    + (pu * w1) * g4[1 - p, 1 - u]
                    + (sp * w2) * swap(g4[1 - p, u])
                )
        for p in range(2):
            r = p * 16
            hs[d, r : r + 16, 0:128] = h[p, 0].astype(BF16)
            hs[d, r : r + 16, 128:256] = h[p, 1].astype(BF16)
            hs[d, 32 + r : 48 + r, 0:128] = (-w_n1 * h[p, 1]).astype(BF16)
            hs[d, 32 + r : 48 + r, 128:256] = (w_n1 * h[p, 0]).astype(BF16)
            for u in range(2):
                hs[d, 64 + r : 80 + r, u * 128 : u * 128 + 128] = (
                    (w_n2 * sgn) * swap(h[p, u])
                ).astype(BF16)

    for cp in takes[2:]:
        cp.wait()
    give = pltpu.make_async_copy(att, o_att, sem.at[6])
    give.start()

    @pl.loop(0, NB)
    def _(t):
        cols = pl.ds(pl.multiple_of(t * BS, BS), BS)
        basis = bt[:, cols]
        pot = jnp.zeros((16, BS), F32)
        fx = jnp.zeros((16, BS), F32)
        fy = jnp.zeros((16, BS), F32)
        fz = jnp.zeros((16, BS), F32)
        for d in range(NI):
            r = nn(hs[d], basis)
            xc = xt[0, d : d + 1, cols]
            xs = xt[1, d : d + 1, cols]
            pot += xc * r[0:16] + xs * r[16:32]
            if d:
                fx += (d * xs) * r[0:16] - (d * xc) * r[16:32]
            fy += xc * r[32:48] + xs * r[48:64]
            fz += xc * r[64:80] + xs * r[80:96]
        o_pot[:, cols] = pot
        ch = chg[:, cols]
        for i, f in enumerate((fx, fy, fz)):
            o_for[i : i + 1, cols] = jnp.sum(ch * f, axis=0, keepdims=True)

    give.wait()


def local(queries, key_states, value_states, fractional, block_counts, neighbors, integer_wave_vectors, charge_weight):
    n_atoms = queries.shape[2]
    vmem = pl.BlockSpec(memory_space=pltpu.VMEM)
    hbm = pl.BlockSpec(memory_space=pltpu.HBM)
    dma = pltpu.SemaphoreType.DMA
    att_shape = jax.ShapeDtypeStruct((25, 16, n_atoms), BF16)
    passed = (
        jax.ShapeDtypeStruct((NI, NG, 8, 128), F32),
        jax.ShapeDtypeStruct((4, 8, 128), F32),
        jax.ShapeDtypeStruct((2, 8, n_atoms), F32),
        jax.ShapeDtypeStruct((256, n_atoms), BF16),
        jax.ShapeDtypeStruct((16, n_atoms), F32),
    )
    slots = [pltpu.VMEM(t.shape, t.dtype) for t in passed]
    made = pl.pallas_call(
        kernel,
        out_shape=(att_shape,) + passed,
        in_specs=[hbm] * 8,
        out_specs=(hbm,) * 6,
        scratch_shapes=[pltpu.VMEM(att_shape.shape, BF16)]
        + slots
        + [
            dma((6,)),
            pltpu.VMEM((1, 16, n_atoms), BF16),
            pltpu.VMEM((1, 16, n_atoms), BF16),
            pltpu.VMEM((3, n_atoms), F32),
            pltpu.SMEM(block_counts.shape, jnp.int32),
            pltpu.SMEM((NNB, NB), jnp.int32),
            pltpu.VMEM(integer_wave_vectors.shape, jnp.int32),
            pltpu.VMEM((16, 16), BF16),
            dma((7,)),
            pltpu.VMEM((NB + 4, 25, 16, BS), BF16),
            pltpu.VMEM((16, n_atoms), BF16),
            pltpu.VMEM((NB, 48, BS), BF16),
            pltpu.VMEM((4, 48, BS), BF16),
            pltpu.VMEM((NB + 4, 48, BS), BF16),
            pltpu.VMEM((NB, 32, BS), BF16),
            pltpu.VMEM((NB, NNB, BS, BS), BF16),
            pltpu.VMEM((NB, 1, BS), F32),
            pltpu.VMEM((NI, NB, 16, BS), BF16),
            pltpu.VMEM((NI, 16, 16), BF16),
            pltpu.VMEM((NG, 8, 128), F32),
            pltpu.VMEM((NG, 8, 128), F32),
            pltpu.VMEM((NR, 8, 128), F32),
            dma((NB,)),
            dma,
            pltpu.SemaphoreType.REGULAR((3,)),
            dma((4,)),
            dma((4,)),
            dma((2, NX - 1)),
            dma((2, NX - 1)),
            dma((2, NX)),
            dma((2, NX)),
            dma((NI - 1,)),
            dma((NI - 1,)),
            dma((NG - 1,)),
            dma((NG - 1,)),
            dma((NR - 1,)),
            dma((NR - 1,)),
            dma((NG - 1,)),
            dma((NG - 1,)),
            dma((NX - 1,)),
            dma((NX - 1,)),
            dma((NX,)),
            dma((NX,)),
        ],
        compiler_params=pltpu.CompilerParams(
            collective_id=0, has_side_effects=True, vmem_limit_bytes=56 << 20
        ),
    )(
        queries,
        key_states,
        fractional,
        block_counts,
        neighbors.T,
        integer_wave_vectors,
        charge_weight,
        value_states.transpose(1, 0, 2),
    )
    attention, potential, forces = pl.pallas_call(
        field,
        out_shape=(
            att_shape,
            jax.ShapeDtypeStruct((16, n_atoms), F32),
            jax.ShapeDtypeStruct((3, n_atoms), F32),
        ),
        in_specs=[hbm] * 6,
        out_specs=(hbm, vmem, vmem),
        scratch_shapes=[pltpu.VMEM(att_shape.shape, BF16)]
        + slots
        + [pltpu.VMEM((NI, 96, 256), BF16), dma((7,))],
        compiler_params=pltpu.CompilerParams(vmem_limit_bytes=56 << 20),
    )(*made)
    return attention.transpose(1, 0, 2), potential, forces


def solution(mesh):
    torus = Mesh(mesh.devices.reshape(NY, NZ, NX, NC), ("y", "z", "x", "c"))
    return jax.shard_map(
        local,
        mesh=torus,
        in_specs=(
            P(INNER, None, SEQ),
            P(INNER, None, SEQ),
            P(INNER, None, SEQ),
            P(None, SEQ),
            P(),
            P(SEQ, None),
            P(),
            P(INNER, None),
        ),
        out_specs=(P(INNER, None, SEQ), P(None, SEQ), P(None, SEQ)),
        check_vma=False,
    )
```

time: 82.2 us -> 68.2 us (0.83)
  Pallas kernels: 74.6 us -> 67.3 us
  local copies, waits for them, and re-layouts: 6.57 us -> 0 us
    pallas_call x1 -> x2, Pallas kernels: 74.6 us -> 67.3 us  [the longest x1 62 us: local(): pl.pallas_call(kernel, out_shape=(att_shape,) + passed, in_specs=[hbm] *...]
    unnamed x17 -> x0, local copies, waits for them, and re-layouts: 6.57 us -> none
where the time goes in v2:
time: 68.2 us; the launch traced here: 68 us
  Pallas kernels  67.3 us (99%)
    pallas_call x1, Pallas kernels, local(): pl.pallas_call(kernel, out_shape=(att_shape,) + passed, in_specs=[hbm] *...  62 us
    pallas_call x1, Pallas kernels, local(): pl.pallas_call(field, out_shape=(att_shape, jax.ShapeDtypeStruct((16, n_a...  5.32 us

profile of v2, /device:TPU:1, one launch (start us, length us, event | category | flops | bytes accessed | tf_op | source)
XLA Modules:
  0.0 68.0 jit_solution(4450695651081698533)
XLA Ops:
  0.6 62.0 %shard_map.103 = (bf16[25,16,2048]{2,1,0:T(8,128)(2,1)}, f32[8,8,8,128]{3,2,1,0:T(8,128)}, f32[4,8,128]{2,1,0:T(8,128)}, f32[2,8,2048]{2,1,0:T(8,128)}, bf16[256,2048]{1,0:T(8,128)(2,1)}, /*index=5*/f32[16,2048]{1,0:T(8,128)}) custom-call(bf16[1,16,2048]{2,1,0:T(8,128)(2,1)} %q_hbm.1, bf16[1,16,2048]{2,1,0:T(8,128)(2,1)} %k_hbm.1, f32[3,2048]{1,0:T(4,128)} %frac_hbm.1, ...), custom_call_target="tpu_custom_call" | custom-call | tf_op jit(solution)/shard_map/pallas_call | solution.py:447
  62.6 5.3 %shard_map.104 = (bf16[25,16,2048]{2,1,0:T(8,128)(2,1)}, f32[16,2048]{1,0:T(8,128)}, f32[3,2048]{1,0:T(4,128)}) custom-call(bf16[25,16,2048]{2,1,0:T(8,128)(2,1)} %get-tuple-element.12.att_hbm, f32[8,8,8,128]{3,2,1,0:T(8,128)} %get-tuple-element.13.gt_hbm, f32[4,8,128]{2,1,0:T(8,128)} %get-tuple-element.14.wt_hbm, f32[2,8,2048]{2,1,0:T(8,128)} %get-tuple-element.15.xt_hbm, ...), custom_call_target="tpu_custom_call" | custom-call | tf_op jit(solution)/shard_map/pallas_call | solution.py:512

commit v3 on v2

--- a/solution.py
+++ b/solution.py
@@ -246,32 +246,34 @@
     store(0, bt, bt_hbm)
     store(1, xt, xt_hbm)
 
-    pass_on(1, out1, on1)
-    for cp in cws + on0:
-        cp.wait_recv()
-
     def charge(at):
         g = (at + 2) % NB
         r = tn(cwa[...].reshape(NI * 16, 16), a0[:, at].reshape(NI * 16, BS))
         chg[:, g * BS : (g + 1) * BS] = r
 
+    def structure(low, high):
+        cols = slice(low * BS, high * BS)
+        charges = chg[:, cols]
+        own_c = xt[0, pl.ds(inner, 1), cols]
+        own_s = xt[1, pl.ds(inner, 1), cols]
+        amp = jnp.concatenate([charges * own_c, charges * own_s], axis=0) * (1.0 / 512.0)
+        amp_h = amp.astype(BF16)
+        amp_l = (amp - amp_h.astype(F32)).astype(BF16)
+        both = nt(jnp.concatenate([amp_h, amp_l], axis=0), bt[:, cols])
+        return both[0:32] + both[32:64]
+
+    for cp in cws + on0:
+        cp.wait_recv()
     for at in range(4):
         charge(at)
+    part = structure(2, 6)
+    pass_on(1, out1, on1)
     for cp in on1:
         cp.wait_recv()
     for at in range(4, 8):
         charge(at)
-
+    part += structure(0, 2) + structure(6, 8)
     store(2, chg, chg_hbm)
-
-    charges = chg[...]
-    own_c = xt[0, pl.ds(inner, 1), :]
-    own_s = xt[1, pl.ds(inner, 1), :]
-    amp = jnp.concatenate([charges * own_c, charges * own_s], axis=0) * (1.0 / 512.0)
-    amp_h = amp.astype(BF16)
-    amp_l = (amp - amp_h.astype(F32)).astype(BF16)
-    both = nt(jnp.concatenate([amp_h, amp_l], axis=0), bt[...])
-    part = both[0:32] + both[32:64]
     for p in range(8):
         gs[p] = part[(p // 2) * 8 : (p // 2) * 8 + 8, (p % 2) * 128 : (p % 2) * 128 + 128]
 
@@ -286,7 +288,7 @@
     os_[rid] = jnp.sum(rs[...], axis=0)
     fsend = [
         send(os_.at[rid], os_.at[rid], f_s.at[o - 1], f_r.at[o - 1], ring_peer(o))
-        for o in range(1, NR)
+        for o in sorted(range(1, NR), key=lambda o: abs(o - NR // 2))
     ]
 
     n0, n1, n2 = iwv[0:1, :], iwv[1:2, :], iwv[2:3, :]
@@ -400,21 +402,19 @@
                     (w_n2 * sgn) * swap(h[p, u])
                 ).astype(BF16)
 
-    for cp in takes[2:]:
-        cp.wait()
-    give = pltpu.make_async_copy(att, o_att, sem.at[6])
-    give.start()
-
-    @pl.loop(0, NB)
-    def _(t):
+    for cp in takes[2:5]:
+        cp.wait()
+
+    def part(t):
         cols = pl.ds(pl.multiple_of(t * BS, BS), BS)
         basis = bt[:, cols]
         pot = jnp.zeros((16, BS), F32)
         fx = jnp.zeros((16, BS), F32)
         fy = jnp.zeros((16, BS), F32)
         fz = jnp.zeros((16, BS), F32)
+        every = nn(hs[...].reshape(NI * 96, 256), basis)
         for d in range(NI):
-            r = nn(hs[d], basis)
+            r = every[d * 96 : (d + 1) * 96]
             xc = xt[0, d : d + 1, cols]
             xs = xt[1, d : d + 1, cols]
             pot += xc * r[0:16] + xs * r[16:32]
@@ -427,6 +427,11 @@
         for i, f in enumerate((fx, fy, fz)):
             o_for[i : i + 1, cols] = jnp.sum(ch * f, axis=0, keepdims=True)
 
+    pl.loop(0, NB // 2)(part)
+    takes[5].wait()
+    give = pltpu.make_async_copy(att, o_att, sem.at[6])
+    give.start()
+    pl.loop(NB // 2, NB)(part)
     give.wait()
 
 

time: 68.2 us -> 66.1 us (0.969)
  Pallas kernels: 67.3 us -> 65.3 us
    pallas_call x1, Pallas kernels: 62 us -> 60.8 us  [local(): pl.pallas_call(kernel, out_shape=(att_shape,) + passed, in_specs=[hbm] *...]
    pallas_call x1, Pallas kernels: 5.32 us -> 4.43 us  [local(): pl.pallas_call(field, out_shape=(att_shape, jax.ShapeDtypeStruct((16, n_a...]
where the time goes in v3:
time: 66.1 us; the launch traced here: 65.9 us
  Pallas kernels  65.3 us (99%)
    pallas_call x1, Pallas kernels, local(): pl.pallas_call(kernel, out_shape=(att_shape,) + passed, in_specs=[hbm] *...  60.8 us
    pallas_call x1, Pallas kernels, local(): pl.pallas_call(field, out_shape=(att_shape, jax.ShapeDtypeStruct((16, n_a...  4.43 us

profile of v3, /device:TPU:1, one launch (start us, length us, event | category | flops | bytes accessed | tf_op | source)
XLA Modules:
  0.0 65.9 jit_solution(14499585693523214818)
XLA Ops:
  0.6 60.8 %shard_map.103 = (bf16[25,16,2048]{2,1,0:T(8,128)(2,1)}, f32[8,8,8,128]{3,2,1,0:T(8,128)}, f32[4,8,128]{2,1,0:T(8,128)}, f32[2,8,2048]{2,1,0:T(8,128)}, bf16[256,2048]{1,0:T(8,128)(2,1)}, /*index=5*/f32[16,2048]{1,0:T(8,128)}) custom-call(bf16[1,16,2048]{2,1,0:T(8,128)(2,1)} %q_hbm.1, bf16[1,16,2048]{2,1,0:T(8,128)(2,1)} %k_hbm.1, f32[3,2048]{1,0:T(4,128)} %frac_hbm.1, ...), custom_call_target="tpu_custom_call" | custom-call | tf_op jit(solution)/shard_map/pallas_call | solution.py:452
  61.5 4.4 %shard_map.104 = (bf16[25,16,2048]{2,1,0:T(8,128)(2,1)}, f32[16,2048]{1,0:T(8,128)}, f32[3,2048]{1,0:T(4,128)}) custom-call(bf16[25,16,2048]{2,1,0:T(8,128)(2,1)} %get-tuple-element.12.att_hbm, f32[8,8,8,128]{3,2,1,0:T(8,128)} %get-tuple-element.13.gt_hbm, f32[4,8,128]{2,1,0:T(8,128)} %get-tuple-element.14.wt_hbm, f32[2,8,2048]{2,1,0:T(8,128)} %get-tuple-element.15.xt_hbm, ...), custom_call_target="tpu_custom_call" | custom-call | tf_op jit(solution)/shard_map/pallas_call | solution.py:517

commit v4 on v3

--- a/solution.py
+++ b/solution.py
@@ -122,23 +122,22 @@
         cp.start()
         loads.append(cp)
 
-    for cp in takes[:5]:
+    for cp in takes[:2]:
         cp.wait()
 
     row16 = lax.broadcasted_iota(jnp.int32, (16, BS), 0)
     lane16 = lax.broadcasted_iota(jnp.int32, (16, BS), 1)
-    for b in range(NB):
+    def build(b):
         cols = pl.ds(b * BS, BS)
         live = lane16 < counts[first + b]
         bias = jnp.where((row16 == 0) & jnp.logical_not(live), DEAD, 0.0)
         ks[b, 0:16, :] = k[0, :, cols]
         ks[b, 16:32, :] = bias.astype(BF16)
-        qs[b, 0:16, :] = (q[0, :, cols].astype(F32) * 0.25).astype(BF16)
-        qs[b, 16:32, :] = jnp.where(row16 == 0, 1.0, 0.0).astype(BF16)
-    cwa[inner] = cw[...]
+        ks[b, 32:48, :] = v0[:, b * BS : (b + 1) * BS]
+
     load_v0.wait()
-    for b in range(NB):
-        ks[b, 32:48, :] = v0[:, b * BS : (b + 1) * BS]
+    for b in (0, 1, 6, 7):
+        build(b)
 
     def send(src, dst, ssem, rsem, dev):
         cp = pltpu.make_async_remote_copy(
@@ -153,10 +152,18 @@
         send(ks.at[pl.ds(0, 2)], kin.at[pl.ds(2, 2)], halo_s.at[1], halo_r.at[1], left),
     ]
     tell(0)
+    for cp in takes[2:5]:
+        cp.wait()
+    cwa[inner] = cw[...]
     cws = [
         send(cwa.at[inner], cwa.at[inner], c_s.at[o - 1], c_r.at[o - 1], inner_peer(o))
         for o in range(1, NI)
     ]
+    for b in (2, 3, 4, 5):
+        build(b)
+    for b in range(NB):
+        qs[b, 0:16, :] = (q[0, :, b * BS : (b + 1) * BS].astype(F32) * 0.25).astype(BF16)
+        qs[b, 16:32, :] = jnp.where(row16 == 0, 1.0, 0.0).astype(BF16)
     for cp in loads[:4]:
         cp.wait()
     vh = [
@@ -185,18 +192,20 @@
         rden[g] = rd
         a0[inner, at] = (acc * rd).astype(BF16)
 
-    def spread(half):
-        mine = a0.at[inner, pl.ds(4 * half, 4)]
-        out = [send(mine, mine, a_s.at[half, o - 1], a_r.at[half, o - 1], x_peer(o)) for o in range(1, NX)]
-        return out, [send(mine, mine, af_s.at[half, 0], af_r.at[half, 0], other)]
-
-    def pass_on(half, out, on):
+    pieces = (pl.ds(0, 4), pl.ds(4, 2), pl.ds(6, 2))
+
+    def spread(i):
+        mine = a0.at[inner, pieces[i]]
+        out = [send(mine, mine, a_s.at[i, o - 1], a_r.at[i, o - 1], x_peer(o)) for o in range(1, NX)]
+        return out, [send(mine, mine, af_s.at[i, 0], af_r.at[i, 0], other)]
+
+    def pass_on(i, out, on):
         for o in range(1, NX):
             out[o - 1].wait_recv()
-            got = a0.at[x_from(o), pl.ds(4 * half, 4)]
-            on.append(send(got, got, af_s.at[half, o], af_r.at[half, o], other))
-
-    @pl.loop(0, 4)
+            got = a0.at[x_from(o), pieces[i]]
+            on.append(send(got, got, af_s.at[i, o], af_r.at[i, o], other))
+
+    @pl.loop(0, 4, unroll=2)
     def _(at):
         attend(ks, first, NB - 1, at)
 
@@ -209,11 +218,17 @@
     kb[2:10] = ks[...]
     kb[10:12] = kin[2:4]
 
-    @pl.loop(4, 8)
+    @pl.loop(4, 6, unroll=2)
     def _(at):
         attend(kb, first - 2, NB + 3, at)
 
     out1, on1 = spread(1)
+
+    @pl.loop(6, 8, unroll=2)
+    def _(at):
+        attend(kb, first - 2, NB + 3, at)
+
+    out2, on2 = spread(2)
     pass_on(0, out0, on0)
     hear(1)
     tell(2)
@@ -268,7 +283,8 @@
         charge(at)
     part = structure(2, 6)
     pass_on(1, out1, on1)
-    for cp in on1:
+    pass_on(2, out2, on2)
+    for cp in on1 + on2:
         cp.wait_recv()
     for at in range(4, 8):
         charge(at)
@@ -340,15 +356,18 @@
     for cp in tsend:
         cp.wait_recv()
     gsend = [send(gt.at[inner], gt.at[inner], g_s.at[o - 1], g_r.at[o - 1], x_peer(o)) for o in range(1, NX)]
+    store(5, gt.at[inner], gt_hbm.at[inner])
     gon = [send(gt.at[inner], gt.at[inner], gf_s.at[0], gf_r.at[0], other)]
     for o in range(1, NX):
         gsend[o - 1].wait_recv()
         got = gt.at[x_from(o)]
         gon.append(send(got, got, gf_s.at[o], gf_r.at[o], other))
-    for cp in gon:
-        cp.wait_recv()
-    store(5, gt, gt_hbm)
-    for cp in kh + cws + vh + out0 + on0 + out1 + on1 + rsend + fsend + tsend + gsend + gon:
+        store(5 + o, got, gt_hbm.at[x_from(o)])
+    for o, cp in enumerate(gon):
+        cp.wait_recv()
+        away = x_from(o) + 1 - 2 * c
+        store(9 + o, gt.at[away], gt_hbm.at[away])
+    for cp in kh + cws + vh + out0 + on0 + out1 + on1 + out2 + on2 + rsend + fsend + tsend + gsend + gon:
         cp.wait_send()
     for cp in stored:
         cp.wait()
@@ -427,11 +446,11 @@
         for i, f in enumerate((fx, fy, fz)):
             o_for[i : i + 1, cols] = jnp.sum(ch * f, axis=0, keepdims=True)
 
-    pl.loop(0, NB // 2)(part)
+    pl.loop(0, 2, unroll=2)(part)
     takes[5].wait()
     give = pltpu.make_async_copy(att, o_att, sem.at[6])
     give.start()
-    pl.loop(NB // 2, NB)(part)
+    pl.loop(2, NB, unroll=2)(part)
     give.wait()
 
 
@@ -457,7 +476,7 @@
         scratch_shapes=[pltpu.VMEM(att_shape.shape, BF16)]
         + slots
         + [
-            dma((6,)),
+            dma((13,)),
             pltpu.VMEM((1, 16, n_atoms), BF16),
             pltpu.VMEM((1, 16, n_atoms), BF16),
             pltpu.VMEM((3, n_atoms), F32),
@@ -484,10 +503,10 @@
             pltpu.SemaphoreType.REGULAR((3,)),
             dma((4,)),
             dma((4,)),
-            dma((2, NX - 1)),
-            dma((2, NX - 1)),
-            dma((2, NX)),
-            dma((2, NX)),
+            dma((3, NX - 1)),
+            dma((3, NX - 1)),
+            dma((3, NX)),
+            dma((3, NX)),
             dma((NI - 1,)),
             dma((NI - 1,)),
             dma((NG - 1,)),

time: 66.1 us -> 65.2 us (0.986)
  Pallas kernels: 65.3 us -> 64.3 us
where the time goes in v4:
time: 65.2 us; the launch traced here: 65 us
  Pallas kernels  64.3 us (99%)
    pallas_call x1, Pallas kernels, local(): pl.pallas_call(kernel, out_shape=(att_shape,) + passed, in_specs=[hbm] *...  60.5 us
    pallas_call x1, Pallas kernels, local(): pl.pallas_call(field, out_shape=(att_shape, jax.ShapeDtypeStruct((16, n_a...  3.86 us

profile of v4, /device:TPU:1, one launch (start us, length us, event | category | flops | bytes accessed | tf_op | source)
XLA Modules:
  0.0 65.0 jit_solution(6567015676830605060)
XLA Ops:
  0.6 60.5 %shard_map.103 = (bf16[25,16,2048]{2,1,0:T(8,128)(2,1)}, f32[8,8,8,128]{3,2,1,0:T(8,128)}, f32[4,8,128]{2,1,0:T(8,128)}, f32[2,8,2048]{2,1,0:T(8,128)}, bf16[256,2048]{1,0:T(8,128)(2,1)}, /*index=5*/f32[16,2048]{1,0:T(8,128)}) custom-call(bf16[1,16,2048]{2,1,0:T(8,128)(2,1)} %q_hbm.1, bf16[1,16,2048]{2,1,0:T(8,128)(2,1)} %k_hbm.1, f32[3,2048]{1,0:T(4,128)} %frac_hbm.1, ...), custom_call_target="tpu_custom_call" | custom-call | tf_op jit(solution)/shard_map/pallas_call | solution.py:471
  61.1 3.9 %shard_map.104 = (bf16[25,16,2048]{2,1,0:T(8,128)(2,1)}, f32[16,2048]{1,0:T(8,128)}, f32[3,2048]{1,0:T(4,128)}) custom-call(bf16[25,16,2048]{2,1,0:T(8,128)(2,1)} %get-tuple-element.12.att_hbm, f32[8,8,8,128]{3,2,1,0:T(8,128)} %get-tuple-element.13.gt_hbm, f32[4,8,128]{2,1,0:T(8,128)} %get-tuple-element.14.wt_hbm, f32[2,8,2048]{2,1,0:T(8,128)} %get-tuple-element.15.xt_hbm, ...), custom_call_target="tpu_custom_call" | custom-call | tf_op jit(solution)/shard_map/pallas_call | solution.py:536

commit v5 on v4

--- a/solution.py
+++ b/solution.py
@@ -353,13 +353,17 @@
         send(gt.at[inner, gid], gt.at[inner, gid], t_s.at[o - 1], t_r.at[o - 1], group_peer(o)[1])
         for o in range(1, NG)
     ]
-    for cp in tsend:
-        cp.wait_recv()
-    gsend = [send(gt.at[inner], gt.at[inner], g_s.at[o - 1], g_r.at[o - 1], x_peer(o)) for o in range(1, NX)]
+    gsend = []
+    for i in range(NG):
+        if i:
+            tsend[i - 1].wait_recv()
+        got = gt.at[inner, lax.rem(gid + NG - i, NG)]
+        gsend.append([send(got, got, g_s.at[i, o - 1], g_r.at[i, o - 1], x_peer(o)) for o in range(1, NX)])
     store(5, gt.at[inner], gt_hbm.at[inner])
     gon = [send(gt.at[inner], gt.at[inner], gf_s.at[0], gf_r.at[0], other)]
     for o in range(1, NX):
-        gsend[o - 1].wait_recv()
+        for sent in gsend:
+            sent[o - 1].wait_recv()
         got = gt.at[x_from(o)]
         gon.append(send(got, got, gf_s.at[o], gf_r.at[o], other))
         store(5 + o, got, gt_hbm.at[x_from(o)])
@@ -367,7 +371,7 @@
         cp.wait_recv()
         away = x_from(o) + 1 - 2 * c
         store(9 + o, gt.at[away], gt_hbm.at[away])
-    for cp in kh + cws + vh + out0 + on0 + out1 + on1 + out2 + on2 + rsend + fsend + tsend + gsend + gon:
+    for cp in kh + cws + vh + out0 + on0 + out1 + on1 + out2 + on2 + rsend + fsend + tsend + sum(gsend, []) + gon:
         cp.wait_send()
     for cp in stored:
         cp.wait()
@@ -515,8 +519,8 @@
             dma((NR - 1,)),
             dma((NG - 1,)),
             dma((NG - 1,)),
-            dma((NX - 1,)),
-            dma((NX - 1,)),
+            dma((NG, NX - 1)),
+            dma((NG, NX - 1)),
             dma((NX,)),
             dma((NX,)),
         ],

time: 65.2 us -> 65.3 us (level)
  no operation moved by 1% of the time
where the time goes in v5:
time: 65.3 us; the launch traced here: 65.1 us
  Pallas kernels  64.4 us (99%)
    pallas_call x1, Pallas kernels, local(): pl.pallas_call(kernel, out_shape=(att_shape,) + passed, in_specs=[hbm] *...  60.6 us
    pallas_call x1, Pallas kernels, local(): pl.pallas_call(field, out_shape=(att_shape, jax.ShapeDtypeStruct((16, n_a...  3.85 us

profile of v5, /device:TPU:1, one launch (start us, length us, event | category | flops | bytes accessed | tf_op | source)
XLA Modules:
  0.0 65.1 jit_solution(1049032559959662992)
XLA Ops:
  0.6 60.6 %shard_map.103 = (bf16[25,16,2048]{2,1,0:T(8,128)(2,1)}, f32[8,8,8,128]{3,2,1,0:T(8,128)}, f32[4,8,128]{2,1,0:T(8,128)}, f32[2,8,2048]{2,1,0:T(8,128)}, bf16[256,2048]{1,0:T(8,128)(2,1)}, /*index=5*/f32[16,2048]{1,0:T(8,128)}) custom-call(bf16[1,16,2048]{2,1,0:T(8,128)(2,1)} %q_hbm.1, bf16[1,16,2048]{2,1,0:T(8,128)(2,1)} %k_hbm.1, f32[3,2048]{1,0:T(4,128)} %frac_hbm.1, ...), custom_call_target="tpu_custom_call" | custom-call | tf_op jit(solution)/shard_map/pallas_call | solution.py:475
  61.2 3.9 %shard_map.104 = (bf16[25,16,2048]{2,1,0:T(8,128)(2,1)}, f32[16,2048]{1,0:T(8,128)}, f32[3,2048]{1,0:T(4,128)}) custom-call(bf16[25,16,2048]{2,1,0:T(8,128)(2,1)} %get-tuple-element.12.att_hbm, f32[8,8,8,128]{3,2,1,0:T(8,128)} %get-tuple-element.13.gt_hbm, f32[4,8,128]{2,1,0:T(8,128)} %get-tuple-element.14.wt_hbm, f32[2,8,2048]{2,1,0:T(8,128)} %get-tuple-element.15.xt_hbm, ...), custom_call_target="tpu_custom_call" | custom-call | tf_op jit(solution)/shard_map/pallas_call | solution.py:540
